TPU v7x, 32 devices: a whole 2x2x4 slice. The times are simulated.
32 devices in a mesh: groups: 2 (over y), slide: 4 (over x, core), band: 4 (over z).
Axes of the slice: x: 2, y: 2, z: 4, core: 2. Of those that a mesh axis runs over, the one named last changes fastest.
Arguments:
- features: bfloat16 [8, 4, 256, 192], P(('groups', 'slide'), 'band'), parts along dimension 0, may hold values from -6 to 6
- tissue: int32 [8, 4, 2], P(('groups', 'slide'), 'band'), parts along dimension 0, may hold values 0 or 1
- cotangent: bfloat16 [8, 4, 256, 192], P(('groups', 'slide'), None, 'band'), parts along dimension 0, may hold values from -6 to 6
- x_proj: float32 [4, 192, 38], replicated, may hold values from -0.4375 to 0.4375
- dt_proj: float32 [4, 6, 192], replicated, may hold values from -2.5 to 2.5
- dt_bias: float32 [4, 192], replicated, may hold values from -6 to -2
- a_log: float32 [4, 16, 192], replicated, may hold values from 0 to 2.77
- d_skip: float32 [4, 192], replicated, may hold values from 0.5 to 1.5
Outputs:
- mixed: bfloat16 [8, 4, 256, 192], P(('groups', 'slide'), None, 'band'), parts along dimension 0
- grad_features: bfloat16 [8, 4, 256, 192], P(('groups', 'slide'), 'band'), parts along dimension 0
- grad_x_proj: float32 [8, 192, 38], P('groups'), parts along dimension 0
- grad_dt_proj: float32 [8, 6, 192], P('groups'), parts along dimension 0
- grad_dt_bias: float32 [8, 192], P('groups'), parts along dimension 0
- grad_a_log: float32 [8, 16, 192], P('groups'), parts along dimension 0
- grad_d_skip: float32 [8, 192], P('groups'), parts along dimension 0
There are 2 independent parts, one for each index of `groups`. A program takes and returns all parts, laid end to end along the dimension named above; an argument that names none is the same for every part. Nothing has to cross between parts.
Inputs may be any that keep to these rules, and one draw needn't show every extreme that they name: 1 marks a tile of 128 tokens of one row that holds tissue, 0 one without.
All inputs are finite; a program needn't handle non-finite values. No bound on the sum of `tissue` on one device may be relied on, other than what follows from the above.
Results may differ from a plain program's by a relative error of at most 0.015.
Values may be sent and summed in bfloat16 or wider, within the bound.
A program may use at most 192 MiB of HBM per device.

v0:
```python
import functools
import math

import jax
import jax.numpy as jnp
from jax import lax
from jax.experimental import pallas as pl
from jax.experimental.pallas import tpu as pltpu
from jax.sharding import PartitionSpec as P

BF = jnp.bfloat16
F32 = jnp.float32
SUB = 8
LANES = 128
LOG2E = math.log2(math.e)


def up(value, unit):
    return -(-value // unit) * unit


def mm(a, b, dims=((1,), (0,))):
    return lax.dot_general(a.astype(BF), b.astype(BF), (dims, ((), ())), preferred_element_type=F32)


def split(a):
    high = a.astype(BF)
    return high, (a - high.astype(F32)).astype(BF)


def mm_exact_left(a, b):
    high, low = split(b)
    return mm(a, high) + mm(a, low)


def mm_exact_right(a, b):
    high, low = split(a)
    return mm(high, b) + mm(low, b)


def mm_three(a, b):
    high, low = split(a)
    return mm_exact_left(high, b) + mm(low, b)


class Sizes:
    def __init__(self, channels, rank, states, steps, seqs):
        self.C, self.R, self.N = channels, rank, states
        self.CP = up(channels + 1, LANES)
        self.L, self.M = steps, seqs
        self.T = steps * seqs
        self.XR = up(rank + 2 * states, SUB)
        self.DR = up(rank, SUB)
        self.rows = self.XR + self.DR + SUB + up(states, SUB)

    def scratch(self):
        t, cp, n = self.T, self.CP, self.N
        wide, narrow = (t, n * cp), (t, n * LANES)
        shapes = dict(
            a=wide, h=wide, bb=narrow, cb=narrow, qb=narrow, qc=narrow,
            u=(t, cp), m=(t, cp), gy=(t, cp), dt=(t, cp), du=(t, cp), z=(t, cp), p=(t, LANES),
            y=(t, cp), s=(t, cp), dd=(t, cp), dv=(t, cp),
            xw=(2, cp, LANES), dw=(2, LANES, cp), bias=(2, SUB, cp), skip=(2, SUB, cp),
            rate=(2 * n, cp), drate=(SUB, n * cp), edge=(SUB, n * cp),
        )
        return shapes


def load_weights(sz, S, x_ref, d_ref, b_ref, l_ref, k_ref):
    for name in ("xw", "dw", "bias", "skip", "rate"):
        S[name][...] = jnp.zeros_like(S[name])
    for k in range(2):
        S["xw"][k, : sz.C, : sz.R + 2 * sz.N] = x_ref[k]
        S["dw"][k, : sz.R, : sz.C] = d_ref[k]
        S["bias"][k, :, : sz.C] = jnp.broadcast_to(b_ref[k : k + 1, :], (SUB, sz.C))
        S["skip"][k, :, : sz.C] = jnp.broadcast_to(k_ref[k : k + 1, :], (SUB, sz.C))
        S["rate"][k * sz.N : (k + 1) * sz.N, : sz.C] = -jnp.exp(l_ref[k])


def prepare(sz, S, k):
    u = S["u"][...]
    p = mm_exact_left(u, S["xw"][k])
    z = mm_three(p, S["dw"][k]) + S["bias"][k, 0:1, :]
    dt = (jnp.maximum(z, 0.0) + jnp.log1p(jnp.exp(-jnp.abs(z)))) * S["m"][...]
    S["p"][...] = p
    S["z"][...] = z
    S["dt"][...] = dt
    S["du"][...] = dt * u
    row = lax.broadcasted_iota(jnp.int32, (LANES, LANES), 0)
    for n in range(sz.N):
        cut = slice(n * LANES, (n + 1) * LANES)
        S["bb"][:, cut] = mm_exact_right(p, (row == sz.R + n).astype(F32))
        S["cb"][:, cut] = mm_exact_right(p, (row == sz.R + sz.N + n).astype(F32))


def wide(sz, n):
    return slice(n * sz.CP, (n + 1) * sz.CP)


def both(sz, value):
    return jnp.concatenate([value] * (sz.CP // LANES), axis=1)


def fold(sz, value):
    total = value[:, :LANES]
    for at in range(LANES, sz.CP, LANES):
        total = total + value[:, at : at + LANES]
    return total


def rows_of(sz, step, group, backwards):
    place = sz.L - 1 - step if backwards else step
    return pl.ds(pl.multiple_of(place * sz.M + group * SUB, SUB), SUB)


def rate_row(sz, S, k, n):
    return jnp.broadcast_to(S["rate"][k * sz.N + n : k * sz.N + n + 1, :], (SUB, sz.CP))


def b_of(sz, S, name, at, n):
    return both(sz, S[name][at, n * LANES : (n + 1) * LANES])


def shift(sz, value, backwards):
    row = lax.broadcasted_iota(jnp.int32, value.shape, 0)
    if backwards:
        return jnp.where(row == SUB - 1, 0.0, pltpu.roll(value, SUB - 1, 0))
    return jnp.where(row == 0, 0.0, pltpu.roll(value, 1, 0))


def join_chunks(sz, S, k, ends, backwards):
    total = jnp.zeros((SUB, sz.CP), F32)
    for step in range(sz.L):
        total = total + S["dt"][step * SUB : (step + 1) * SUB, :]
    for n in range(sz.N):
        decay = jnp.exp(total * rate_row(sz, S, k, n))
        start = jnp.zeros((SUB, sz.CP), F32)
        for _ in range(SUB - 1):
            start = shift(sz, decay * start + ends[n], backwards)
        S["edge"][:, wide(sz, n)] = start


def zeros(sz):
    return tuple(jnp.zeros((SUB, sz.CP), F32) for _ in range(sz.N))


def edges(sz, S):
    return tuple(S["edge"][:, wide(sz, n)] for n in range(sz.N))


def local_states(sz, S, k):
    rev = k == 1

    def body(i, h):
        at = rows_of(sz, i, 0, rev)
        dt, du = S["dt"][at, :], S["du"][at, :]
        out = []
        for n in range(sz.N):
            a = jnp.exp2(dt * (LOG2E * rate_row(sz, S, k, n)))
            S["a"][at, wide(sz, n)] = a
            out.append(a * h[n] + du * b_of(sz, S, "bb", at, n))
        return tuple(out)

    join_chunks(sz, S, k, lax.fori_loop(0, sz.L, body, zeros(sz)), rev)


def run_states(sz, S, k, group, start, chunked, want_y, want_grad):
    rev = k == 1

    def body(i, h):
        at = rows_of(sz, i, group, rev)
        dt, du = S["dt"][at, :], S["du"][at, :]
        gy = S["gy"][at, :] if want_grad else None
        y = None
        out = []
        for n in range(sz.N):
            if chunked:
                a = S["a"][at, wide(sz, n)]
            else:
                a = jnp.exp2(dt * (LOG2E * rate_row(sz, S, k, n)))
                S["a"][at, wide(sz, n)] = a
            new = a * h[n] + du * b_of(sz, S, "bb", at, n)
            if want_grad:
                S["h"][at, wide(sz, n)] = h[n]
                S["qc"][at, n * LANES : (n + 1) * LANES] = fold(sz, gy * new)
            if want_y:
                term = new * b_of(sz, S, "cb", at, n)
                y = term if y is None else y + term
            out.append(new)
        if want_y:
            S["y"][at, :] = S["y"][at, :] + y + S["skip"][k] * S["u"][at, :]
        return tuple(out)

    lax.fori_loop(0, sz.L, body, start)


def local_adjoints(sz, S, k):
    rev = k == 0

    def body(i, e):
        at = rows_of(sz, i, 0, rev)
        gy = S["gy"][at, :]
        return tuple(
            S["a"][at, wide(sz, n)] * (b_of(sz, S, "cb", at, n) * gy + e[n]) for n in range(sz.N)
        )

    join_chunks(sz, S, k, lax.fori_loop(0, sz.L, body, zeros(sz)), rev)


def run_adjoints(sz, S, k, group, start):
    rev = k == 0

    def body(i, e):
        at = rows_of(sz, i, group, rev)
        gy, dt, du = S["gy"][at, :], S["dt"][at, :], S["du"][at, :]
        s = dd = None
        out = []
        for n in range(sz.N):
            g = b_of(sz, S, "cb", at, n) * gy + e[n]
            w = S["a"][at, wide(sz, n)] * g
            S["qb"][at, n * LANES : (n + 1) * LANES] = fold(sz, g * du)
            sb = g * b_of(sz, S, "bb", at, n)
            t = w * S["h"][at, wide(sz, n)]
            rt = rate_row(sz, S, k, n) * t
            s = sb if s is None else s + sb
            dd = rt if dd is None else dd + rt
            S["drate"][:, wide(sz, n)] = S["drate"][:, wide(sz, n)] + dt * t
            out.append(w)
        S["s"][at, :] = s
        S["dd"][at, :] = dd
        return tuple(out)

    lax.fori_loop(0, sz.L, body, start)


def finish(sz, S, k, g_ref):
    u, m, gy, dt = S["u"][...], S["m"][...], S["gy"][...], S["dt"][...]
    s = S["s"][...]
    dz = (u * s + S["dd"][...]) * m * jax.nn.sigmoid(S["z"][...])
    dp = mm(dz, S["dw"][k], ((1,), (1,)))
    col = lax.broadcasted_iota(jnp.int32, (LANES, LANES), 1)
    for n in range(sz.N):
        cut = slice(n * LANES, (n + 1) * LANES)
        dp = dp + mm(S["qb"][:, cut], (col == sz.R + n).astype(F32))
        dp = dp + mm(S["qc"][:, cut], (col == sz.R + sz.N + n).astype(F32))
    du = dt * s + S["skip"][k, 0:1, :] * gy + mm(dp, S["xw"][k], ((1,), (1,)))
    S["dv"][...] = S["dv"][...] + m * du
    at = sz.XR
    g_ref[k, :at, :] = mm(dp.T, u)[:at]
    g_ref[k, at : at + sz.DR, :] = mm(S["p"][...].T, dz)[: sz.DR]
    at += sz.DR
    g_ref[k, at : at + SUB, :] = jnp.zeros((SUB, sz.CP), F32)
    g_ref[k, at : at + 1, :] = jnp.sum(dz, axis=0, keepdims=True)
    g_ref[k, at + 1 : at + 2, :] = jnp.sum(gy * u, axis=0, keepdims=True)
    at += SUB
    for n in range(sz.N):
        total = jnp.sum(S["drate"][:, wide(sz, n)], axis=0, keepdims=True)
        g_ref[k, at + n : at + n + 1, :] = total * S["rate"][k * sz.N + n : k * sz.N + n + 1, :]


def place(sz):
    shape = (sz.L, SUB, sz.T)
    step, chunk, token = (lax.broadcasted_iota(jnp.int32, shape, axis) for axis in range(3))
    return (token == chunk * sz.L + step).astype(F32).reshape(sz.T, sz.T)


def row_inputs(sz, S, v_ref, t_ref):
    shape = (sz.L, SUB, sz.CP)
    step, chunk = (lax.broadcasted_iota(jnp.int32, shape, axis) for axis in range(2))
    token = (chunk * sz.L + step).reshape(sz.T, sz.CP)
    tiles = t_ref.shape[0]
    span = sz.T // tiles
    m = jnp.zeros((sz.T, sz.CP), F32)
    for w in range(tiles):
        inside = (token >= w * span) & (token < (w + 1) * span)
        m = jnp.where(inside, t_ref[w].astype(F32), m)
    S["m"][...] = m
    S["u"][...] = jnp.zeros_like(S["u"])
    S["u"][:, : sz.C] = mm(place(sz), v_ref[...])
    S["u"][...] = S["u"][...] * m


def rows_forward(sz, names, v_ref, t_ref, *rest):
    weights, out_ref, S = rest[:5], rest[5], dict(zip(names, rest[6:]))
    load_weights(sz, S, *weights)
    row_inputs(sz, S, v_ref, t_ref)
    S["y"][...] = jnp.zeros_like(S["y"])
    for k in range(2):
        prepare(sz, S, k)
        local_states(sz, S, k)
        run_states(sz, S, k, 0, edges(sz, S), True, True, False)
    lane = lax.broadcasted_iota(jnp.int32, (sz.T, sz.CP), 1)
    y = jnp.where(lane == sz.C, S["m"][...], S["y"][...])
    out_ref[...] = mm(place(sz), y, ((0,), (0,))).astype(BF)


def columns_both(sz, names, v_ref, c_ref, *rest):
    weights, out_ref, grad_ref, g_ref, S = rest[:5], rest[5], rest[6], rest[7], dict(zip(names, rest[8:]))
    load_weights(sz, S, *weights)
    v = v_ref[...].astype(F32)
    lane = lax.broadcasted_iota(jnp.int32, (sz.T, sz.CP), 1)
    m = jnp.broadcast_to(v[:, sz.C : sz.C + 1], (sz.T, sz.CP))
    S["m"][...] = m
    S["u"][...] = jnp.where(lane < sz.C, v, 0.0) * m
    S["gy"][...] = jnp.zeros_like(S["gy"])
    S["gy"][:, : sz.C] = c_ref[...].astype(F32)
    S["y"][...] = jnp.zeros_like(S["y"])
    S["dv"][...] = jnp.zeros_like(S["dv"])
    for k in range(2):
        prepare(sz, S, k)
        S["drate"][...] = jnp.zeros_like(S["drate"])

        def group_body(group, carry):
            run_states(sz, S, k, group, zeros(sz), False, True, True)
            run_adjoints(sz, S, k, group, zeros(sz))
            return carry

        lax.fori_loop(0, sz.M // SUB, group_body, 0)
        finish(sz, S, k, g_ref)
    out_ref[...] = S["y"][:, : sz.C].astype(BF)
    grad_ref[...] = S["dv"][...].astype(BF)


def rows_backward(sz, names, v_ref, t_ref, c_ref, *rest):
    weights, out_ref, g_ref, S = rest[:5], rest[5], rest[6], dict(zip(names, rest[7:]))
    load_weights(sz, S, *weights)
    row_inputs(sz, S, v_ref, t_ref)
    S["gy"][...] = mm(place(sz), c_ref[...])
    S["dv"][...] = jnp.zeros_like(S["dv"])
    for k in range(2):
        prepare(sz, S, k)
        S["drate"][...] = jnp.zeros_like(S["drate"])
        local_states(sz, S, k)
        run_states(sz, S, k, 0, edges(sz, S), True, False, True)
        local_adjoints(sz, S, k)
        run_adjoints(sz, S, k, 0, edges(sz, S))
        finish(sz, S, k, g_ref)
    out_ref[...] = mm(place(sz), S["dv"][...], ((0,), (0,)))[:, : sz.C].astype(BF)


def call(body, sz, out_shape, n_vmem_first, has_tissue, args, name):
    shapes = sz.scratch()
    specs = [pl.BlockSpec(memory_space=pltpu.VMEM)] * len(args)
    if has_tissue:
        specs[1] = pl.BlockSpec(memory_space=pltpu.SMEM)
    return pl.pallas_call(
        functools.partial(body, sz, tuple(shapes)),
        out_shape=out_shape,
        in_specs=specs,
        out_specs=jax.tree.map(lambda _: pl.BlockSpec(memory_space=pltpu.VMEM), out_shape),
        scratch_shapes=[pltpu.VMEM(shape, F32) for shape in shapes.values()],
        compiler_params=pltpu.CompilerParams(vmem_limit_bytes=56 * 1024 * 1024),
        name=name,
    )(*args)


def reduce_all(packed, axes):
    count = lax.axis_size(axes)
    size = packed.size
    each = up(size, count) // count
    flat = packed.reshape(-1)
    if each * count != size:
        flat = jnp.pad(flat, (0, each * count - size))
    parts = lax.all_to_all(flat.reshape(count, each), axes, split_axis=0, concat_axis=0, tiled=True)
    mine = jnp.broadcast_to(jnp.sum(parts, axis=0)[None], (count, each))
    gathered = lax.all_to_all(mine, axes, split_axis=0, concat_axis=0, tiled=True)
    return gathered.reshape(-1)[:size].reshape(packed.shape)


def shards(features, tissue, cotangent, x_proj, dt_proj, dt_bias, a_log, d_skip):
    local_slides, local_rows, width, channels = features.shape
    assert local_slides == 1 and local_rows == 1
    bands = lax.axis_size("band")
    cols = width // bands
    rank, states = dt_proj.shape[1], a_log.shape[1]
    weights = (x_proj, dt_proj, dt_bias, a_log, d_skip)
    horiz = tuple(weight[:2] for weight in weights)
    vert = tuple(weight[2:] for weight in weights)
    rz = Sizes(channels, rank, states, width // SUB, SUB)
    cz = Sizes(channels, rank, states, bands, cols)
    v = features.reshape(width, channels)
    t = tissue.reshape(-1)
    shape = jax.ShapeDtypeStruct
    carried = call(rows_forward, rz, shape((width, rz.CP), BF), 0, True, (v, t) + horiz, "rows_forward")
    moved = lax.all_to_all(carried.reshape(bands, cols, rz.CP), "band", split_axis=0, concat_axis=0, tiled=True)
    mixed, grad_cols, grads_v = call(
        columns_both, cz,
        (shape((cz.T, channels), BF), shape((cz.T, cz.CP), BF), shape((2, cz.rows, cz.CP), F32)),
        0, False, (moved.reshape(cz.T, cz.CP), cotangent.reshape(cz.T, channels)) + vert, "columns",
    )
    back = lax.all_to_all(grad_cols.reshape(bands, cols, cz.CP), "band", split_axis=0, concat_axis=0, tiled=True)
    grad_rows, grads_h = call(
        rows_backward, rz,
        (shape((width, channels), BF), shape((2, rz.rows, rz.CP), F32)),
        0, True, (v, t, back.reshape(width, rz.CP)) + horiz, "rows_backward",
    )
    packed = jnp.concatenate([grads_h, grads_v], axis=0)
    total = reduce_all(packed, ("slide", "band"))
    at = rz.XR + rz.DR
    return (
        mixed.reshape(cotangent.shape),
        grad_rows.reshape(features.shape),
        jnp.swapaxes(total[:, : rank + 2 * states, :channels], 1, 2),
        total[:, rz.XR : rz.XR + rank, :channels],
        total[:, at, :channels],
        total[:, at + SUB : at + SUB + states, :channels],
        total[:, at + 1, :channels],
    )


def solution(mesh):
    in_specs = (
        P(("groups", "slide"), "band", None, None),
        P(("groups", "slide"), "band", None),
        P(("groups", "slide"), None, "band", None),
        P(), P(), P(), P(), P(),
    )
    out_specs = (
        P(("groups", "slide"), None, "band", None),
        P(("groups", "slide"), "band", None, None),
        P("groups", None, None),
        P("groups", None, None),
        P("groups", None),
        P("groups", None, None),
        P("groups", None),
    )
    return jax.shard_map(shards, mesh=mesh, in_specs=in_specs, out_specs=out_specs, check_vma=False)
```

profile of v0, /device:TPU:0, one launch (start us, length us, event | category | flops | bytes accessed | tf_op | source)
XLA Modules:
  0.0 105.4 jit_solution(12741610047875948851)
XLA Ops:
  0.7 0.8 fusion.3
  1.5 0.6 copy.42.rest_1_
  2.1 0.6 fusion.2
  2.7 0.8 copy.30
  3.6 0.8 copy.41.rest_0_
  5.0 10.6 %rows_forward.1 = bf16[256,256]{1,0:T(8,128)(2,1)} custom-call(bf16[256,192]{1,0:T(8,128)(2,1)} %bitcast.17, s32[2]{0:T(128)} %bitcast.27, f32[2,192,38]{2,1,0:T(8,128)} %copy.41.rest_0_, f32[2,6,192]{2,1,0:T(8,128)} %copy.42.rest_1_, f32[2,192]{1,0:T(2,128)} %get-tuple-element.50.rest_2_, f32[2,16,192]{2,1,0:T(8,128)} %get-tuple-element.43.rest_3_, ...), custom_call_target="tpu_custom_call" | custom-call | tf_op jit(solution)/shard_map/rows_forward/pallas_call | solution.py:346
  15.6 6.3 %all-to-all-start = ((bf16[4,64,256]{2,1,0:T(8,128)(2,1)}), bf16[4,64,256]{2,1,0:T(8,128)(2,1)S(1)}, u32[]{:S(2)}, u32[]{:S(2)}) async-start(bf16[4,64,256]{2,1,0:T(8,128)(2,1)} %bitcast.19), calls=%async_computation | async-start | bytes 262144 | tf_op jit(solution)/shard_map/all_to_all | solution.py:385
  22.0 0.6 copy.44.rest_1_
  22.6 0.8 copy.43.rest_0_
  23.4 4.7 %all-to-all-done = bf16[4,64,256]{2,1,0:T(8,128)(2,1)S(1)} async-done(((bf16[4,64,256]{2,1,0:T(8,128)(2,1)}), bf16[4,64,256]{2,1,0:T(8,128)(2,1)S(1)}, u32[]{:S(2)}, u32[]{:S(2)}) %all-to-all-start) | async-done | bytes 131104 | tf_op jit(solution)/shard_map/all_to_all | solution.py:385
  28.0 0.6 copy-done
  28.7 14.3 %columns.1 = (bf16[256,192]{1,0:T(8,128)(2,1)}, bf16[256,256]{1,0:T(8,128)(2,1)}, f32[2,72,256]{2,1,0:T(8,128)}) custom-call(bf16[256,256]{1,0:T(8,128)(2,1)} %bitcast.21, bf16[256,192]{1,0:T(8,128)(2,1)} %bitcast.24, f32[2,192,38]{2,1,0:T(8,128)} %copy.43.rest_0_, f32[2,6,192]{2,1,0:T(8,128)} %copy.44.rest_1_, f32[2,192]{1,0:T(2,128)} %get-tuple-element.51.rest_2_, ...), custom_call_target="tpu_custom_call" | custom-call | tf_op jit(solution)/shard_map/columns/pallas_call | solution.py:346
  42.9 9.9 %all_to_all.26 = bf16[4,64,256]{2,1,0:T(8,128)(2,1)} all-to-all(bf16[4,64,256]{2,1,0:T(8,128)(2,1)} %bitcast.23), channel_id=1, replica_groups=mesh['groups'=2,'slide'=4,'band'=4] {'band'}, dimensions={0} | all-to-all | bytes 262144 | tf_op jit(solution)/shard_map/all_to_all | solution.py:391
  52.8 17.4 %rows_backward.1 = (bf16[256,192]{1,0:T(8,128)(2,1)}, f32[2,72,256]{2,1,0:T(8,128)}) custom-call(bf16[256,192]{1,0:T(8,128)(2,1)} %bitcast.18, s32[2]{0:T(128)} %bitcast.28, bf16[256,256]{1,0:T(8,128)(2,1)} %bitcast.20, f32[2,192,38]{2,1,0:T(8,128)} %copy.41.rest_0_, f32[2,6,192]{2,1,0:T(8,128)} %copy.42.rest_1_, f32[2,192]{1,0:T(2,128)} %get-tuple-element.50.rest_2_, ...), custom_call_target="tpu_custom_call" | custom-call | tf_op jit(solution)/shard_map/rows_backward/pallas_call | solution.py:346
  70.3 0.9 pad_maximum_fusion
  71.5 14.5 %all_to_all.27 = f32[16,1,4608]{2,1,0:T(1,128)S(1)} all-to-all(f32[16,1,4608]{2,1,0:T(1,128)S(1)} %all_to_all.21), channel_id=1, replica_groups=mesh['groups'=2,'slide'=4,'band'=4] {'slide','band'}, dimensions={0} | all-to-all | bytes 589824 | tf_op jit(solution)/shard_map/all_to_all | solution.py:364
  86.2 0.9 broadcast_in_dim.2
  87.0 3.7 %all-to-all-start.3 = ((f32[16,1,4608]{2,1,0:T(1,128)}), f32[16,1,4608]{2,1,0:T(1,128)S(1)}, u32[]{:S(2)}, u32[]{:S(2)}) async-start(f32[16,1,4608]{2,1,0:T(1,128)} %broadcast_in_dim.2), calls=%async_computation.3 | async-start | bytes 589824 | tf_op jit(solution)/shard_map/all_to_all | solution.py:366
  90.7 0.7 copy.36
  91.5 10.0 %all-to-all-done.3 = f32[16,1,4608]{2,1,0:T(1,128)S(1)} async-done(((f32[16,1,4608]{2,1,0:T(1,128)}), f32[16,1,4608]{2,1,0:T(1,128)S(1)}, u32[]{:S(2)}, u32[]{:S(2)}) %all-to-all-start.3) | async-done | bytes 294944 | tf_op jit(solution)/shard_map/all_to_all | solution.py:366
  101.4 0.7 reduce.1
  102.2 0.6 slice.63
  104.1 0.6 copy.38
  104.7 0.7 copy.37
  (25 shorter events, 2.5 us)
Async XLA Ops:
  0.6 1.5 %copy-start.5 = (f32[4,16,192]{2,1,0:T(8,128)S(1)}, f32[4,16,192]{2,1,0:T(8,128)}, u32[]{:S(2)}) copy-start(f32[4,16,192]{2,1,0:T(8,128)} %param.14) | copy-start | bytes 147460
  0.6 2.1 %copy-start.4 = (bf16[1,1,256,192]{2,3,1,0:T(8,128)(2,1)S(1)}, bf16[1,1,256,192]{2,3,1,0:T(8,128)(2,1)}, u32[]{:S(2)}) copy-start(bf16[1,1,256,192]{2,3,1,0:T(8,128)(2,1)} %param.8) | copy-start | bytes 294916
  2.1 1.4 %copy-start.1 = (f32[4,192,38]{1,0,2:T(4,128)S(1)}, f32[4,192,38]{1,0,2:T(4,128)}, u32[]{:S(2)}) copy-start(f32[4,192,38]{1,0,2:T(4,128)} %param.11) | copy-start | bytes 350212
  3.5 0.8 copy-start.6
  3.6 0.8 copy-start.7
  15.6 12.4 %all-to-all-start = ((bf16[4,64,256]{2,1,0:T(8,128)(2,1)}), bf16[4,64,256]{2,1,0:T(8,128)(2,1)S(1)}, u32[]{:S(2)}, u32[]{:S(2)}) async-start(bf16[4,64,256]{2,1,0:T(8,128)(2,1)} %bitcast.19), calls=%async_computation | async-start | bytes 262144 | tf_op jit(solution)/shard_map/all_to_all | solution.py:385
  28.0 0.6 copy-start
  52.8 17.4 %copy-start.2 = (f32[2,72,256]{2,1,0:T(8,128)S(1)}, f32[2,72,256]{2,1,0:T(8,128)}, u32[]{:S(2)}) copy-start(f32[2,72,256]{2,1,0:T(8,128)} %get-tuple-element.16) | copy-start | bytes 442372
  87.0 3.7 %copy-start.3 = (bf16[256,192]{1,0:T(8,128)(2,1)S(1)}, bf16[256,192]{1,0:T(8,128)(2,1)}, u32[]{:S(2)}) copy-start(bf16[256,192]{1,0:T(8,128)(2,1)} %get-tuple-element.14) | copy-start | bytes 294916
  87.0 14.4 %all-to-all-start.3 = ((f32[16,1,4608]{2,1,0:T(1,128)}), f32[16,1,4608]{2,1,0:T(1,128)S(1)}, u32[]{:S(2)}, u32[]{:S(2)}) async-start(f32[16,1,4608]{2,1,0:T(1,128)} %broadcast_in_dim.2), calls=%async_computation.3 | async-start | bytes 589824 | tf_op jit(solution)/shard_map/all_to_all | solution.py:366
where the time goes:
time: 106 us; the launch traced here: 105 us
  Pallas kernels  42.3 us (40%)
  blocking collectives  24.4 us (23%)
  waiting for transfers between devices  14.6 us (14%)
  local copies, waits for them, and re-layouts  11.5 us (11%)
  starting transfers between devices  9.99 us (9%)
  other arithmetic  1.81 us (2%)
    pallas_call x3, Pallas kernels, call(): pl.pallas_call(functools.partial(body, sz, tuple(shapes)), out_shape=out_...  42.3 us
    all_to_all x1, blocking collectives, reduce_all(): lax.all_to_all(flat.reshape(count, each), axes, split_axis=0, concat_axis...  14.5 us
    all_to_all x1, waiting for transfers between devices, reduce_all(): lax.all_to_all(mine, axes, split_axis=0, concat_axis=0, tiled=True)  9.97 us
    all_to_all x1, blocking collectives, shards(): lax.all_to_all(grad_cols.reshape(bands, cols, cz.CP), 'band', split_axis=...  9.92 us
    unnamed x26, local copies, waits for them, and re-layouts  7.54 us
    all_to_all x1, starting transfers between devices, shards(): lax.all_to_all(carried.reshape(bands, cols, rz.CP), 'band', split_axis=0,...  6.32 us
    all_to_all x1, waiting for transfers between devices, shards(): lax.all_to_all(carried.reshape(bands, cols, rz.CP), 'band', split_axis=0,...  4.65 us
    all_to_all x1, starting transfers between devices, reduce_all(): lax.all_to_all(mine, axes, split_axis=0, concat_axis=0, tiled=True)  3.67 us
  transfers between devices with their start and end apart: 2, of which 2 were waited for; matrix products, arithmetic and copies ran while one was open for 2% of the time, Pallas kernels for 0%

commit v1 on v0

--- a/solution.py
+++ b/solution.py
@@ -51,7 +51,7 @@
         self.T = steps * seqs
         self.XR = up(rank + 2 * states, SUB)
         self.DR = up(rank, SUB)
-        self.rows = self.XR + self.DR + SUB + up(states, SUB)
+        self.rows = up(self.XR + self.DR + SUB + up(states, SUB), 2 * SUB)
 
     def scratch(self):
         t, cp, n = self.T, self.CP, self.N
@@ -66,15 +66,15 @@
         return shapes
 
 
-def load_weights(sz, S, x_ref, d_ref, b_ref, l_ref, k_ref):
+def load_weights(sz, S, base, x_ref, d_ref, b_ref, l_ref, k_ref):
     for name in ("xw", "dw", "bias", "skip", "rate"):
         S[name][...] = jnp.zeros_like(S[name])
     for k in range(2):
-        S["xw"][k, : sz.C, : sz.R + 2 * sz.N] = x_ref[k]
-        S["dw"][k, : sz.R, : sz.C] = d_ref[k]
-        S["bias"][k, :, : sz.C] = jnp.broadcast_to(b_ref[k : k + 1, :], (SUB, sz.C))
-        S["skip"][k, :, : sz.C] = jnp.broadcast_to(k_ref[k : k + 1, :], (SUB, sz.C))
-        S["rate"][k * sz.N : (k + 1) * sz.N, : sz.C] = -jnp.exp(l_ref[k])
+        S["xw"][k, : sz.C, : sz.R + 2 * sz.N] = x_ref[base + k]
+        S["dw"][k, : sz.R, : sz.C] = d_ref[base + k]
+        S["bias"][k, :, : sz.C] = jnp.broadcast_to(b_ref[base + k : base + k + 1, :], (SUB, sz.C))
+        S["skip"][k, :, : sz.C] = jnp.broadcast_to(k_ref[base + k : base + k + 1, :], (SUB, sz.C))
+        S["rate"][k * sz.N : (k + 1) * sz.N, : sz.C] = -jnp.exp(l_ref[base + k])
 
 
 def prepare(sz, S, k):
@@ -246,10 +246,10 @@
     du = dt * s + S["skip"][k, 0:1, :] * gy + mm(dp, S["xw"][k], ((1,), (1,)))
     S["dv"][...] = S["dv"][...] + m * du
     at = sz.XR
+    g_ref[k, :, :] = jnp.zeros((sz.rows, sz.CP), F32)
     g_ref[k, :at, :] = mm(dp.T, u)[:at]
     g_ref[k, at : at + sz.DR, :] = mm(S["p"][...].T, dz)[: sz.DR]
     at += sz.DR
-    g_ref[k, at : at + SUB, :] = jnp.zeros((SUB, sz.CP), F32)
     g_ref[k, at : at + 1, :] = jnp.sum(dz, axis=0, keepdims=True)
     g_ref[k, at + 1 : at + 2, :] = jnp.sum(gy * u, axis=0, keepdims=True)
     at += SUB
@@ -282,7 +282,7 @@
 
 def rows_forward(sz, names, v_ref, t_ref, *rest):
     weights, out_ref, S = rest[:5], rest[5], dict(zip(names, rest[6:]))
-    load_weights(sz, S, *weights)
+    load_weights(sz, S, 0, *weights)
     row_inputs(sz, S, v_ref, t_ref)
     S["y"][...] = jnp.zeros_like(S["y"])
     for k in range(2):
@@ -296,7 +296,7 @@
 
 def columns_both(sz, names, v_ref, c_ref, *rest):
     weights, out_ref, grad_ref, g_ref, S = rest[:5], rest[5], rest[6], rest[7], dict(zip(names, rest[8:]))
-    load_weights(sz, S, *weights)
+    load_weights(sz, S, 2, *weights)
     v = v_ref[...].astype(F32)
     lane = lax.broadcasted_iota(jnp.int32, (sz.T, sz.CP), 1)
     m = jnp.broadcast_to(v[:, sz.C : sz.C + 1], (sz.T, sz.CP))
@@ -323,7 +323,7 @@
 
 def rows_backward(sz, names, v_ref, t_ref, c_ref, *rest):
     weights, out_ref, g_ref, S = rest[:5], rest[5], rest[6], dict(zip(names, rest[7:]))
-    load_weights(sz, S, *weights)
+    load_weights(sz, S, 0, *weights)
     row_inputs(sz, S, v_ref, t_ref)
     S["gy"][...] = mm(place(sz), c_ref[...])
     S["dv"][...] = jnp.zeros_like(S["dv"])
@@ -354,17 +354,113 @@
     )(*args)
 
 
-def reduce_all(packed, axes):
-    count = lax.axis_size(axes)
-    size = packed.size
-    each = up(size, count) // count
-    flat = packed.reshape(-1)
-    if each * count != size:
-        flat = jnp.pad(flat, (0, each * count - size))
-    parts = lax.all_to_all(flat.reshape(count, each), axes, split_axis=0, concat_axis=0, tiled=True)
-    mine = jnp.broadcast_to(jnp.sum(parts, axis=0)[None], (count, each))
-    gathered = lax.all_to_all(mine, axes, split_axis=0, concat_axis=0, tiled=True)
-    return gathered.reshape(-1)[:size].reshape(packed.shape)
+def greet(sides):
+    barrier = pltpu.get_barrier_semaphore()
+    total = 0
+    for axis, count in sides:
+        me = lax.axis_index(axis)
+        for off in range(1, count):
+            pl.semaphore_signal(
+                barrier, inc=1, device_id={axis: lax.rem(me + off, count)},
+                device_id_type=pl.DeviceIdType.MESH,
+            )
+        total += count - 1
+    pl.semaphore_wait(barrier, total)
+
+
+def spread(axis, count, source_of, land, send_sem, recv_sem):
+    me = lax.axis_index(axis)
+    copies = []
+    for off in range(1, count):
+        other = lax.rem(me + off, count)
+        copies.append(
+            pltpu.make_async_remote_copy(
+                src_ref=source_of(other), dst_ref=land.at[me],
+                send_sem=send_sem.at[off], recv_sem=recv_sem.at[off],
+                device_id={axis: other}, device_id_type=pl.DeviceIdType.MESH,
+            )
+        )
+    for copy in copies:
+        copy.start()
+    return copies
+
+
+def exchange_body(count, in_ref, out_ref, land, send_sem, recv_sem):
+    greet((("band", count),))
+    me = lax.axis_index("band")
+    copies = spread("band", count, lambda other: in_ref.at[other], land, send_sem, recv_sem)
+    land[me] = in_ref[me]
+    for copy in copies:
+        copy.wait()
+    out_ref[...] = land[...]
+
+
+def exchange(blocks, ident):
+    count = lax.axis_size("band")
+    return pl.pallas_call(
+        functools.partial(exchange_body, count),
+        out_shape=jax.ShapeDtypeStruct(blocks.shape, blocks.dtype),
+        in_specs=[pl.BlockSpec(memory_space=pltpu.VMEM)],
+        out_specs=pl.BlockSpec(memory_space=pltpu.VMEM),
+        scratch_shapes=[
+            pltpu.VMEM(blocks.shape, blocks.dtype),
+            pltpu.SemaphoreType.DMA((count,)),
+            pltpu.SemaphoreType.DMA((count,)),
+        ],
+        compiler_params=pltpu.CompilerParams(collective_id=ident, has_side_effects=True),
+        name="band_exchange",
+    )(blocks)
+
+
+def reduce_body(slides, bands, each, h_ref, v_ref, out_ref, pack, land, part, every, total, whole, *sems):
+    greet((("slide", slides), ("band", bands)))
+    slide, band = lax.axis_index("slide"), lax.axis_index("band")
+    rows = h_ref.shape[1]
+    flat = 2 * h_ref.shape[0] * rows
+    values = [ref[k] for ref in (h_ref, v_ref) for k in range(ref.shape[0])]
+    spare = slides * each - flat
+    if spare:
+        values.append(jnp.zeros((spare, h_ref.shape[2]), F32))
+    pack[...] = jnp.concatenate(values, axis=0).astype(BF).reshape(pack.shape)
+    copies = spread("slide", slides, lambda other: pack.at[other], land, sems[0], sems[1])
+    land[slide] = pack[slide]
+    for copy in copies:
+        copy.wait()
+    part[...] = sum(land[at].astype(F32) for at in range(slides)).astype(BF)
+    copies = spread("band", bands, lambda other: part, every, sems[2], sems[3])
+    every[band] = part[...]
+    for copy in copies:
+        copy.wait()
+    total[...] = sum(every[at].astype(F32) for at in range(bands)).astype(BF)
+    copies = spread("slide", slides, lambda other: total, whole, sems[4], sems[5])
+    whole[slide] = total[...]
+    for copy in copies:
+        copy.wait()
+    out_ref[...] = whole[...].astype(F32)
+
+
+def reduce_all(grads_h, grads_v):
+    slides, bands = lax.axis_size("slide"), lax.axis_size("band")
+    half, rows, lanes = grads_h.shape
+    each = up(up(2 * half * rows, slides) // slides, 2 * SUB)
+    block = (each, lanes)
+    out = pl.pallas_call(
+        functools.partial(reduce_body, slides, bands, each),
+        out_shape=jax.ShapeDtypeStruct((slides,) + block, F32),
+        in_specs=[pl.BlockSpec(memory_space=pltpu.VMEM)] * 2,
+        out_specs=pl.BlockSpec(memory_space=pltpu.VMEM),
+        scratch_shapes=[
+            pltpu.VMEM((slides,) + block, BF), pltpu.VMEM((slides,) + block, BF),
+            pltpu.VMEM(block, BF), pltpu.VMEM((bands,) + block, BF),
+            pltpu.VMEM(block, BF), pltpu.VMEM((slides,) + block, BF),
+        ]
+        + [pltpu.SemaphoreType.DMA((count,)) for count in (slides, slides, bands, bands, slides, slides)],
+        compiler_params=pltpu.CompilerParams(
+            collective_id=2, has_side_effects=True, vmem_limit_bytes=32 * 1024 * 1024
+        ),
+        name="gradient_sum",
+    )(grads_h, grads_v)
+    return out.reshape(slides * each, lanes)[: 2 * half * rows].reshape(2 * half, rows, lanes)
 
 
 def shards(features, tissue, cotangent, x_proj, dt_proj, dt_bias, a_log, d_skip):
@@ -374,28 +470,25 @@
     cols = width // bands
     rank, states = dt_proj.shape[1], a_log.shape[1]
     weights = (x_proj, dt_proj, dt_bias, a_log, d_skip)
-    horiz = tuple(weight[:2] for weight in weights)
-    vert = tuple(weight[2:] for weight in weights)
     rz = Sizes(channels, rank, states, width // SUB, SUB)
     cz = Sizes(channels, rank, states, bands, cols)
     v = features.reshape(width, channels)
     t = tissue.reshape(-1)
     shape = jax.ShapeDtypeStruct
-    carried = call(rows_forward, rz, shape((width, rz.CP), BF), 0, True, (v, t) + horiz, "rows_forward")
-    moved = lax.all_to_all(carried.reshape(bands, cols, rz.CP), "band", split_axis=0, concat_axis=0, tiled=True)
+    carried = call(rows_forward, rz, shape((width, rz.CP), BF), 0, True, (v, t) + weights, "rows_forward")
+    moved = exchange(carried.reshape(bands, cols, rz.CP), 0)
     mixed, grad_cols, grads_v = call(
         columns_both, cz,
         (shape((cz.T, channels), BF), shape((cz.T, cz.CP), BF), shape((2, cz.rows, cz.CP), F32)),
-        0, False, (moved.reshape(cz.T, cz.CP), cotangent.reshape(cz.T, channels)) + vert, "columns",
+        0, False, (moved.reshape(cz.T, cz.CP), cotangent.reshape(cz.T, channels)) + weights, "columns",
     )
-    back = lax.all_to_all(grad_cols.reshape(bands, cols, cz.CP), "band", split_axis=0, concat_axis=0, tiled=True)
+    back = exchange(grad_cols.reshape(bands, cols, cz.CP), 1)
     grad_rows, grads_h = call(
         rows_backward, rz,
         (shape((width, channels), BF), shape((2, rz.rows, rz.CP), F32)),
-        0, True, (v, t, back.reshape(width, rz.CP)) + horiz, "rows_backward",
+        0, True, (v, t, back.reshape(width, rz.CP)) + weights, "rows_backward",
     )
-    packed = jnp.concatenate([grads_h, grads_v], axis=0)
-    total = reduce_all(packed, ("slide", "band"))
+    total = reduce_all(grads_h, grads_v)
     at = rz.XR + rz.DR
     return (
         mixed.reshape(cotangent.shape),

time: 106 us -> 84.8 us (0.80)
  Pallas kernels: 42.3 us -> 74.5 us
  blocking collectives: 24.4 us -> 0 us
  waiting for transfers between devices: 14.6 us -> 0 us
  starting transfers between devices: 9.99 us -> 0 us
  local copies, waits for them, and re-layouts: 11.5 us -> 9.24 us
  other arithmetic: 1.81 us -> 0 us
    pallas_call x0 -> x3, Pallas kernels: none -> 32 us  [the longest x2 18.1 us: exchange(): pl.pallas_call(functools.partial(exchange_body, count), out_shape=jax.Sha...]
    all_to_all x2 -> x0, blocking collectives: 24.4 us -> none  [the longest x1 14.5 us: reduce_all(): lax.all_to_all(flat.reshape(count, each), axes, split_axis=0, concat_axis...]
    all_to_all x2 -> x0, waiting for transfers between devices: 14.6 us -> none  [the longest x1 9.97 us: reduce_all(): lax.all_to_all(mine, axes, split_axis=0, concat_axis=0, tiled=True)]
    all_to_all x2 -> x0, starting transfers between devices: 9.99 us -> none  [the longest x1 6.32 us: shards(): lax.all_to_all(carried.reshape(bands, cols, rz.CP), 'band', split_axis=0,...]
    slice x4 -> x0, local copies, waits for them, and re-layouts: 2.12 us -> none  [shards(): vert = tuple((weight[2:] for weight in weights))]
    unnamed x26 -> x13, local copies, waits for them, and re-layouts: 7.54 us -> 8.58 us
  transfers between devices with their start and end apart: 2 -> 0, of which waited for: 2 -> 0; matrix products, arithmetic and copies ran while one was open for 2% -> 0% of each run, Pallas kernels for 0% -> 0%
where the time goes in v1:
time: 84.8 us; the launch traced here: 84.5 us
  Pallas kernels  74.5 us (88%)
  local copies, waits for them, and re-layouts  9.24 us (11%)
    pallas_call x3, Pallas kernels, call(): pl.pallas_call(functools.partial(body, sz, tuple(shapes)), out_shape=out_...  42.5 us
    pallas_call x2, Pallas kernels, exchange(): pl.pallas_call(functools.partial(exchange_body, count), out_shape=jax.Sha...  18.1 us
    pallas_call x1, Pallas kernels, reduce_all(): pl.pallas_call(functools.partial(reduce_body, slides, bands, each), out_s...  14 us
    unnamed x13, local copies, waits for them, and re-layouts  8.58 us

profile of v1, /device:TPU:0, one launch (start us, length us, event | category | flops | bytes accessed | tf_op | source)
XLA Modules:
  0.0 84.5 jit_solution(16515773983776358708)
XLA Ops:
  0.6 0.0 copy-start.2
  0.6 1.4 %copy.17.rest_1_ = f32[4,6,192]{2,1,0:T(8,128)} copy(f32[4,6,192]{2,0,1:T(4,128)} %param.12) | data formatting | bytes 36864 | tf_op args[4]
  2.0 1.7 %copy.15 = bf16[1,1,256,192]{3,2,1,0:T(8,128)(2,1)} copy(bf16[1,1,256,192]{2,3,1,0:T(8,128)(2,1)} %param.8) | data formatting | bytes 196608 | tf_op args[0]
  3.7 0.0 copy-done.2
  3.7 1.0 %copy.16.rest_0_ = f32[4,192,38]{2,1,0:T(8,128)} copy(f32[4,192,38]{1,0,2:T(4,128)S(1)} %copy-done.2) | data formatting | bytes 233472 | tf_op args[3]
  4.7 10.7 %rows_forward.1 = bf16[256,256]{1,0:T(8,128)(2,1)} custom-call(bf16[256,192]{1,0:T(8,128)(2,1)} %bitcast.15, s32[2]{0:T(128)} %bitcast.23, f32[4,192,38]{2,1,0:T(8,128)} %copy.16.rest_0_, f32[4,6,192]{2,1,0:T(8,128)} %copy.17.rest_1_, f32[4,192]{1,0:T(4,128)} %rest_2_.5, f32[4,16,192]{2,1,0:T(8,128)} %rest_3_.5, f32[4,192]{1,0:T(4,128)} %rest_4_.5), custom_call_target="tpu_custom_call" | custom-call | tf_op jit(solution)/shard_map/rows_forward/pallas_call | solution.py:346
  15.4 10.0 %band_exchange.2 = bf16[4,64,256]{2,1,0:T(8,128)(2,1)} custom-call(bf16[4,64,256]{2,1,0:T(8,128)(2,1)} %bitcast.19), custom_call_target="tpu_custom_call" | custom-call | tf_op jit(solution)/shard_map/band_exchange/pallas_call | solution.py:400
  25.4 14.3 %columns.1 = (bf16[256,192]{1,0:T(8,128)(2,1)}, bf16[256,256]{1,0:T(8,128)(2,1)}, f32[2,80,256]{2,1,0:T(8,128)}) custom-call(bf16[256,256]{1,0:T(8,128)(2,1)} %bitcast.18, bf16[256,192]{1,0:T(8,128)(2,1)} %bitcast.22, f32[4,192,38]{2,1,0:T(8,128)} %copy.16.rest_0_, f32[4,6,192]{2,1,0:T(8,128)} %copy.17.rest_1_, f32[4,192]{1,0:T(4,128)} %rest_2_.5, ...), custom_call_target="tpu_custom_call" | custom-call | tf_op jit(solution)/shard_map/columns/pallas_call | solution.py:346
  39.7 8.0 %band_exchange.3 = bf16[4,64,256]{2,1,0:T(8,128)(2,1)} custom-call(bf16[4,64,256]{2,1,0:T(8,128)(2,1)} %bitcast.21), custom_call_target="tpu_custom_call" | custom-call | tf_op jit(solution)/shard_map/band_exchange/pallas_call | solution.py:400
  47.8 17.4 %rows_backward.1 = (bf16[256,192]{1,0:T(8,128)(2,1)}, f32[2,80,256]{2,1,0:T(8,128)}) custom-call(bf16[256,192]{1,0:T(8,128)(2,1)} %bitcast.16, s32[2]{0:T(128)} %bitcast.24, bf16[256,256]{1,0:T(8,128)(2,1)} %bitcast.17, f32[4,192,38]{2,1,0:T(8,128)} %copy.16.rest_0_, f32[4,6,192]{2,1,0:T(8,128)} %copy.17.rest_1_, f32[4,192]{1,0:T(4,128)} %rest_2_.5, ...), custom_call_target="tpu_custom_call" | custom-call | tf_op jit(solution)/shard_map/rows_backward/pallas_call | solution.py:346
  65.2 0.0 copy-start
  65.2 1.7 %copy.22 = bf16[1,1,256,192]{2,3,1,0:T(8,128)(2,1)} copy(bf16[1,1,256,192]{3,2,1,0:T(8,128)(2,1)} %bitcast.20) | data formatting | bytes 196608
  66.9 0.0 copy-done
  66.9 0.0 copy-start.1
  66.9 0.9 %copy-done.1 = f32[2,80,256]{2,1,0:T(8,128)S(1)} copy-done((f32[2,80,256]{2,1,0:T(8,128)S(1)}, f32[2,80,256]{2,1,0:T(8,128)}, u32[]{:S(2)}) %copy-start.1) | copy-done | bytes 163864
  67.9 14.0 %gradient_sum.1 = f32[4,80,256]{2,1,0:T(8,128)S(1)} custom-call(f32[2,80,256]{2,1,0:T(8,128)S(1)} %copy-done.1, f32[2,80,256]{2,1,0:T(8,128)S(1)} %copy-done), custom_call_target="tpu_custom_call" | custom-call | tf_op jit(solution)/shard_map/gradient_sum/pallas_call | solution.py:447
  81.9 0.6 copy_bitcast_fusion
  82.5 0.6 copy.24
  83.1 0.6 slice.18
  83.7 0.7 copy.23
  (3 shorter events, 0.0 us)
Async XLA Ops:
  0.6 3.1 %copy-start.2 = (f32[4,192,38]{1,0,2:T(4,128)S(1)}, f32[4,192,38]{1,0,2:T(4,128)}, u32[]{:S(2)}) copy-start(f32[4,192,38]{1,0,2:T(4,128)} %param.11) | copy-start | bytes 350212
  65.2 1.7 %copy-start = (f32[2,80,256]{2,1,0:T(8,128)S(1)}, f32[2,80,256]{2,1,0:T(8,128)}, u32[]{:S(2)}) copy-start(f32[2,80,256]{2,1,0:T(8,128)} %get-tuple-element.16.v_ref) | copy-start | bytes 491524
  66.9 0.9 %copy-start.1 = (f32[2,80,256]{2,1,0:T(8,128)S(1)}, f32[2,80,256]{2,1,0:T(8,128)}, u32[]{:S(2)}) copy-start(f32[2,80,256]{2,1,0:T(8,128)} %get-tuple-element.15.h_ref) | copy-start | bytes 491524

commit v2 on v0

--- a/solution.py
+++ b/solution.py
@@ -51,7 +51,7 @@
         self.T = steps * seqs
         self.XR = up(rank + 2 * states, SUB)
         self.DR = up(rank, SUB)
-        self.rows = self.XR + self.DR + SUB + up(states, SUB)
+        self.rows = up(self.XR + self.DR + SUB + up(states, SUB), 2 * SUB)
 
     def scratch(self):
         t, cp, n = self.T, self.CP, self.N
@@ -66,15 +66,15 @@
         return shapes
 
 
-def load_weights(sz, S, x_ref, d_ref, b_ref, l_ref, k_ref):
+def load_weights(sz, S, base, x_ref, d_ref, b_ref, l_ref, k_ref):
     for name in ("xw", "dw", "bias", "skip", "rate"):
         S[name][...] = jnp.zeros_like(S[name])
     for k in range(2):
-        S["xw"][k, : sz.C, : sz.R + 2 * sz.N] = x_ref[k]
-        S["dw"][k, : sz.R, : sz.C] = d_ref[k]
-        S["bias"][k, :, : sz.C] = jnp.broadcast_to(b_ref[k : k + 1, :], (SUB, sz.C))
-        S["skip"][k, :, : sz.C] = jnp.broadcast_to(k_ref[k : k + 1, :], (SUB, sz.C))
-        S["rate"][k * sz.N : (k + 1) * sz.N, : sz.C] = -jnp.exp(l_ref[k])
+        S["xw"][k, : sz.C, : sz.R + 2 * sz.N] = x_ref[base + k]
+        S["dw"][k, : sz.R, : sz.C] = d_ref[base + k]
+        S["bias"][k, :, : sz.C] = jnp.broadcast_to(b_ref[base + k : base + k + 1, :], (SUB, sz.C))
+        S["skip"][k, :, : sz.C] = jnp.broadcast_to(k_ref[base + k : base + k + 1, :], (SUB, sz.C))
+        S["rate"][k * sz.N : (k + 1) * sz.N, : sz.C] = -jnp.exp(l_ref[base + k])
 
 
 def prepare(sz, S, k):
@@ -246,10 +246,10 @@
     du = dt * s + S["skip"][k, 0:1, :] * gy + mm(dp, S["xw"][k], ((1,), (1,)))
     S["dv"][...] = S["dv"][...] + m * du
     at = sz.XR
+    g_ref[k, :, :] = jnp.zeros((sz.rows, sz.CP), F32)
     g_ref[k, :at, :] = mm(dp.T, u)[:at]
     g_ref[k, at : at + sz.DR, :] = mm(S["p"][...].T, dz)[: sz.DR]
     at += sz.DR
-    g_ref[k, at : at + SUB, :] = jnp.zeros((SUB, sz.CP), F32)
     g_ref[k, at : at + 1, :] = jnp.sum(dz, axis=0, keepdims=True)
     g_ref[k, at + 1 : at + 2, :] = jnp.sum(gy * u, axis=0, keepdims=True)
     at += SUB
@@ -276,13 +276,72 @@
         m = jnp.where(inside, t_ref[w].astype(F32), m)
     S["m"][...] = m
     S["u"][...] = jnp.zeros_like(S["u"])
-    S["u"][:, : sz.C] = mm(place(sz), v_ref[...])
+    S["u"][:, : sz.C] = mm(place(sz), v_ref[...], ((1,), (1,)))
     S["u"][...] = S["u"][...] * m
 
 
-def rows_forward(sz, names, v_ref, t_ref, *rest):
+def greet(sides):
+    barrier = pltpu.get_barrier_semaphore()
+    total = 0
+    for axis, count in sides:
+        me = lax.axis_index(axis)
+        for off in range(1, count):
+            pl.semaphore_signal(
+                barrier, inc=1, device_id={axis: lax.rem(me + off, count)},
+                device_id_type=pl.DeviceIdType.MESH,
+            )
+        total += count - 1
+    return lambda: pl.semaphore_wait(barrier, total)
+
+
+def spread(axis, count, source_of, land, send_sem, recv_sem):
+    me = lax.axis_index(axis)
+    copies = []
+    for off in range(1, count):
+        other = lax.rem(me + off, count)
+        copies.append(
+            pltpu.make_async_remote_copy(
+                src_ref=source_of(other), dst_ref=land.at[me],
+                send_sem=send_sem.at[off], recv_sem=recv_sem.at[off],
+                device_id={axis: other}, device_id_type=pl.DeviceIdType.MESH,
+            )
+        )
+    for copy in copies:
+        copy.start()
+    return copies
+
+
+def sum_gradients(slides, bands, each, h_ref, v_ref, out_ref, pack, land, part, every, total, whole, *sems):
+    slide, band = lax.axis_index("slide"), lax.axis_index("band")
+    rows = h_ref.shape[1]
+    flat = 2 * h_ref.shape[0] * rows
+    values = [ref[k] for ref in (h_ref, v_ref) for k in range(ref.shape[0])]
+    spare = slides * each - flat
+    if spare:
+        values.append(jnp.zeros((spare, h_ref.shape[2]), F32))
+    pack[...] = jnp.concatenate(values, axis=0).astype(BF).reshape(pack.shape)
+    copies = spread("slide", slides, lambda other: pack.at[other], land, sems[0], sems[1])
+    land[slide] = pack[slide]
+    for copy in copies:
+        copy.wait()
+    part[...] = sum(land[at].astype(F32) for at in range(slides)).astype(BF)
+    copies = spread("band", bands, lambda other: part, every, sems[2], sems[3])
+    every[band] = part[...]
+    for copy in copies:
+        copy.wait()
+    total[...] = sum(every[at].astype(F32) for at in range(bands)).astype(BF)
+    copies = spread("slide", slides, lambda other: total, whole, sems[4], sems[5])
+    whole[slide] = total[...]
+    for copy in copies:
+        copy.wait()
+    out_ref[...] = whole[...].astype(F32)
+
+
+def rows_forward(bands, sz, names, v_ref, t_ref, *rest):
     weights, out_ref, S = rest[:5], rest[5], dict(zip(names, rest[6:]))
-    load_weights(sz, S, *weights)
+    block, land, send_sem, recv_sem = rest[6 + len(names) :]
+    arrived = greet((("band", bands),))
+    load_weights(sz, S, 0, *weights)
     row_inputs(sz, S, v_ref, t_ref)
     S["y"][...] = jnp.zeros_like(S["y"])
     for k in range(2):
@@ -291,12 +350,19 @@
         run_states(sz, S, k, 0, edges(sz, S), True, True, False)
     lane = lax.broadcasted_iota(jnp.int32, (sz.T, sz.CP), 1)
     y = jnp.where(lane == sz.C, S["m"][...], S["y"][...])
-    out_ref[...] = mm(place(sz), y, ((0,), (0,))).astype(BF)
+    block[...] = mm(place(sz), y, ((0,), (0,))).astype(BF).reshape(block.shape)
+    arrived()
+    me = lax.axis_index("band")
+    copies = spread("band", bands, lambda other: block.at[other], land, send_sem, recv_sem)
+    land[me] = block[me]
+    for copy in copies:
+        copy.wait()
+    out_ref[...] = land[...]
 
 
 def columns_both(sz, names, v_ref, c_ref, *rest):
     weights, out_ref, grad_ref, g_ref, S = rest[:5], rest[5], rest[6], rest[7], dict(zip(names, rest[8:]))
-    load_weights(sz, S, *weights)
+    load_weights(sz, S, 2, *weights)
     v = v_ref[...].astype(F32)
     lane = lax.broadcasted_iota(jnp.int32, (sz.T, sz.CP), 1)
     m = jnp.broadcast_to(v[:, sz.C : sz.C + 1], (sz.T, sz.CP))
@@ -321,24 +387,34 @@
     grad_ref[...] = S["dv"][...].astype(BF)
 
 
-def rows_backward(sz, names, v_ref, t_ref, c_ref, *rest):
-    weights, out_ref, g_ref, S = rest[:5], rest[5], rest[6], dict(zip(names, rest[7:]))
-    load_weights(sz, S, *weights)
+def rows_backward(slides, bands, each, sz, names, v_ref, t_ref, c_ref, gv_ref, *rest):
+    weights, out_ref, sum_ref, S = rest[:5], rest[5], rest[6], dict(zip(names, rest[7:]))
+    land, send_sem, recv_sem, g_ref, *summing = rest[7 + len(names) :]
+    arrived = greet((("slide", slides), ("band", bands)))
+    load_weights(sz, S, 0, *weights)
     row_inputs(sz, S, v_ref, t_ref)
-    S["gy"][...] = mm(place(sz), c_ref[...])
     S["dv"][...] = jnp.zeros_like(S["dv"])
+    arrived()
+    me = lax.axis_index("band")
+    copies = spread("band", bands, lambda other: c_ref.at[other], land, send_sem, recv_sem)
+    land[me] = c_ref[me]
     for k in range(2):
         prepare(sz, S, k)
         S["drate"][...] = jnp.zeros_like(S["drate"])
         local_states(sz, S, k)
+        if k == 0:
+            for copy in copies:
+                copy.wait()
+            S["gy"][...] = mm(place(sz), land[...].reshape(sz.T, sz.CP))
         run_states(sz, S, k, 0, edges(sz, S), True, False, True)
         local_adjoints(sz, S, k)
         run_adjoints(sz, S, k, 0, edges(sz, S))
         finish(sz, S, k, g_ref)
-    out_ref[...] = mm(place(sz), S["dv"][...], ((0,), (0,)))[:, : sz.C].astype(BF)
-
-
-def call(body, sz, out_shape, n_vmem_first, has_tissue, args, name):
+    out_ref[...] = mm(S["dv"][...], place(sz), ((0,), (0,)))[: sz.C].astype(BF)
+    sum_gradients(slides, bands, each, g_ref, gv_ref, sum_ref, *summing)
+
+
+def call(body, sz, out_shape, has_tissue, args, name, extra=(), ident=None):
     shapes = sz.scratch()
     specs = [pl.BlockSpec(memory_space=pltpu.VMEM)] * len(args)
     if has_tissue:
@@ -348,23 +424,12 @@
         out_shape=out_shape,
         in_specs=specs,
         out_specs=jax.tree.map(lambda _: pl.BlockSpec(memory_space=pltpu.VMEM), out_shape),
-        scratch_shapes=[pltpu.VMEM(shape, F32) for shape in shapes.values()],
-        compiler_params=pltpu.CompilerParams(vmem_limit_bytes=56 * 1024 * 1024),
+        scratch_shapes=[pltpu.VMEM(shape, F32) for shape in shapes.values()] + list(extra),
+        compiler_params=pltpu.CompilerParams(
+            vmem_limit_bytes=56 * 1024 * 1024, collective_id=ident, has_side_effects=ident is not None
+        ),
         name=name,
     )(*args)
-
-
-def reduce_all(packed, axes):
-    count = lax.axis_size(axes)
-    size = packed.size
-    each = up(size, count) // count
-    flat = packed.reshape(-1)
-    if each * count != size:
-        flat = jnp.pad(flat, (0, each * count - size))
-    parts = lax.all_to_all(flat.reshape(count, each), axes, split_axis=0, concat_axis=0, tiled=True)
-    mine = jnp.broadcast_to(jnp.sum(parts, axis=0)[None], (count, each))
-    gathered = lax.all_to_all(mine, axes, split_axis=0, concat_axis=0, tiled=True)
-    return gathered.reshape(-1)[:size].reshape(packed.shape)
 
 
 def shards(features, tissue, cotangent, x_proj, dt_proj, dt_bias, a_log, d_skip):
@@ -374,32 +439,43 @@
     cols = width // bands
     rank, states = dt_proj.shape[1], a_log.shape[1]
     weights = (x_proj, dt_proj, dt_bias, a_log, d_skip)
-    horiz = tuple(weight[:2] for weight in weights)
-    vert = tuple(weight[2:] for weight in weights)
     rz = Sizes(channels, rank, states, width // SUB, SUB)
     cz = Sizes(channels, rank, states, bands, cols)
-    v = features.reshape(width, channels)
+    v = jnp.swapaxes(features.reshape(width, channels), 0, 1)
     t = tissue.reshape(-1)
     shape = jax.ShapeDtypeStruct
-    carried = call(rows_forward, rz, shape((width, rz.CP), BF), 0, True, (v, t) + horiz, "rows_forward")
-    moved = lax.all_to_all(carried.reshape(bands, cols, rz.CP), "band", split_axis=0, concat_axis=0, tiled=True)
+    slides = lax.axis_size("slide")
+    moved_shape = (bands, cols, rz.CP)
+    dma = pltpu.SemaphoreType.DMA
+    moved = call(
+        functools.partial(rows_forward, bands), rz, shape(moved_shape, BF), True, (v, t) + weights, "rows_forward",
+        [pltpu.VMEM(moved_shape, BF), pltpu.VMEM(moved_shape, BF), dma((bands,)), dma((bands,))], 0,
+    )
     mixed, grad_cols, grads_v = call(
         columns_both, cz,
         (shape((cz.T, channels), BF), shape((cz.T, cz.CP), BF), shape((2, cz.rows, cz.CP), F32)),
-        0, False, (moved.reshape(cz.T, cz.CP), cotangent.reshape(cz.T, channels)) + vert, "columns",
+        False, (moved.reshape(cz.T, cz.CP), cotangent.reshape(cz.T, channels)) + weights, "columns",
     )
-    back = lax.all_to_all(grad_cols.reshape(bands, cols, cz.CP), "band", split_axis=0, concat_axis=0, tiled=True)
-    grad_rows, grads_h = call(
-        rows_backward, rz,
-        (shape((width, channels), BF), shape((2, rz.rows, rz.CP), F32)),
-        0, True, (v, t, back.reshape(width, rz.CP)) + horiz, "rows_backward",
+    each = up(up(4 * rz.rows, slides) // slides, 2 * SUB)
+    block = (each, rz.CP)
+    grad_rows, total = call(
+        functools.partial(rows_backward, slides, bands, each), rz,
+        (shape((channels, width), BF), shape((slides,) + block, F32)),
+        True, (v, t, grad_cols.reshape(moved_shape), grads_v) + weights, "rows_backward",
+        [pltpu.VMEM(moved_shape, BF), dma((bands,)), dma((bands,)), pltpu.VMEM((2, rz.rows, rz.CP), F32)]
+        + [
+            pltpu.VMEM((slides,) + block, BF), pltpu.VMEM((slides,) + block, BF),
+            pltpu.VMEM(block, BF), pltpu.VMEM((bands,) + block, BF),
+            pltpu.VMEM(block, BF), pltpu.VMEM((slides,) + block, BF),
+        ]
+        + [dma((count,)) for count in (slides, slides, bands, bands, slides, slides)],
+        1,
     )
-    packed = jnp.concatenate([grads_h, grads_v], axis=0)
-    total = reduce_all(packed, ("slide", "band"))
+    total = total.reshape(slides * each, rz.CP)[: 4 * rz.rows].reshape(4, rz.rows, rz.CP)
     at = rz.XR + rz.DR
     return (
         mixed.reshape(cotangent.shape),
-        grad_rows.reshape(features.shape),
+        jnp.swapaxes(grad_rows, 0, 1).reshape(features.shape),
         jnp.swapaxes(total[:, : rank + 2 * states, :channels], 1, 2),
         total[:, rz.XR : rz.XR + rank, :channels],
         total[:, at, :channels],

time: 106 us -> 75.6 us (0.71)
  blocking collectives: 24.4 us -> 0 us
  Pallas kernels: 42.3 us -> 64.4 us
  waiting for transfers between devices: 14.6 us -> 0 us
  starting transfers between devices: 9.99 us -> 0 us
  other arithmetic: 1.81 us -> 0 us
  local copies, waits for them, and re-layouts: 11.5 us -> 9.97 us
    all_to_all x2 -> x0, blocking collectives: 24.4 us -> none  [the longest x1 14.5 us: reduce_all(): lax.all_to_all(flat.reshape(count, each), axes, split_axis=0, concat_axis...]
    pallas_call x3, Pallas kernels: 42.3 us -> 64.4 us  [call(): pl.pallas_call(functools.partial(body, sz, tuple(shapes)), out_shape=out_...]
    all_to_all x2 -> x0, waiting for transfers between devices: 14.6 us -> none  [the longest x1 9.97 us: reduce_all(): lax.all_to_all(mine, axes, split_axis=0, concat_axis=0, tiled=True)]
    all_to_all x2 -> x0, starting transfers between devices: 9.99 us -> none  [the longest x1 6.32 us: shards(): lax.all_to_all(carried.reshape(bands, cols, rz.CP), 'band', split_axis=0,...]
    slice x4 -> x0, local copies, waits for them, and re-layouts: 2.12 us -> none  [shards(): vert = tuple((weight[2:] for weight in weights))]
    unnamed x26 -> x8, local copies, waits for them, and re-layouts: 7.54 us -> 5.97 us
  transfers between devices with their start and end apart: 2 -> 0, of which waited for: 2 -> 0; matrix products, arithmetic and copies ran while one was open for 2% -> 0% of each run, Pallas kernels for 0% -> 0%
where the time goes in v2:
time: 75.6 us; the launch traced here: 75.1 us
  Pallas kernels  64.4 us (85%)
  local copies, waits for them, and re-layouts  9.97 us (13%)
    pallas_call x3, Pallas kernels, call(): pl.pallas_call(functools.partial(body, sz, tuple(shapes)), out_shape=out_...  64.4 us
    unnamed x8, local copies, waits for them, and re-layouts  5.97 us

profile of v2, /device:TPU:0, one launch (start us, length us, event | category | flops | bytes accessed | tf_op | source)
XLA Modules:
  0.0 75.1 jit_solution(14884817665357355564)
XLA Ops:
  0.6 1.4 %copy.16.rest_1_ = f32[4,6,192]{2,1,0:T(8,128)} copy(f32[4,6,192]{2,0,1:T(4,128)} %param.12) | data formatting | bytes 36864 | tf_op args[4]
  2.0 1.9 %copy.15.rest_0_ = f32[4,192,38]{2,1,0:T(8,128)} copy(f32[4,192,38]{1,0,2:T(4,128)} %param.11) | data formatting | bytes 233472 | tf_op args[3]
  3.9 18.0 %rows_forward.1 = bf16[4,64,256]{2,1,0:T(8,128)(2,1)} custom-call(bf16[192,256]{1,0:T(8,128)(2,1)} %bitcast.18, s32[2]{0:T(128)} %bitcast.23, f32[4,192,38]{2,1,0:T(8,128)} %copy.15.rest_0_, f32[4,6,192]{2,1,0:T(8,128)} %copy.16.rest_1_, f32[4,192]{1,0:T(4,128)} %rest_2_.5, f32[4,16,192]{2,1,0:T(8,128)} %rest_3_.5, f32[4,192]{1,0:T(4,128)} %rest_4_.5), custom_call_target="tpu_custom_call" | custom-call | tf_op jit(solution)/shard_map/rows_forward/pallas_call | solution.py:422
  21.9 14.3 %columns.1 = (bf16[256,192]{1,0:T(8,128)(2,1)}, bf16[256,256]{1,0:T(8,128)(2,1)}, f32[2,80,256]{2,1,0:T(8,128)}) custom-call(bf16[256,256]{1,0:T(8,128)(2,1)} %bitcast.17, bf16[256,192]{1,0:T(8,128)(2,1)} %bitcast.21, f32[4,192,38]{2,1,0:T(8,128)} %copy.15.rest_0_, f32[4,6,192]{2,1,0:T(8,128)} %copy.16.rest_1_, f32[4,192]{1,0:T(4,128)} %rest_2_.5, ...), custom_call_target="tpu_custom_call" | custom-call | tf_op jit(solution)/shard_map/columns/pallas_call | solution.py:422
  36.2 32.1 %rows_backward.1 = (bf16[192,256]{1,0:T(8,128)(2,1)}, f32[4,80,256]{2,1,0:T(8,128)}) custom-call(bf16[192,256]{1,0:T(8,128)(2,1)} %bitcast.19, s32[2]{0:T(128)} %bitcast.24, bf16[4,64,256]{2,1,0:T(8,128)(2,1)} %bitcast.20, f32[2,80,256]{2,1,0:T(8,128)} %get-tuple-element.14.gv_ref, f32[4,192,38]{2,1,0:T(8,128)} %copy.15.rest_0_, f32[4,6,192]{2,1,0:T(8,128)} %copy.16.rest_1_, ...), custom_call_target="tpu_custom_call" | custom-call | tf_op jit(solution)/shard_map/rows_backward/pallas_call | solution.py:422
  68.3 0.8 %fusion = (f32[4,1,192]{2,1,0:T(1,128)S(1)}, f32[4,1,192]{2,1,0:T(1,128)S(1)}) fusion(f32[4,80,256]{2,1,0:T(8,128)} %get-tuple-element.16), kind=kLoop, calls=%fused_computation.3 | loop fusion | bytes 12288 | tf_op jit(solution)/shard_map/slice | solution.py:483
  69.1 0.6 copy_bitcast_fusion
  69.7 0.8 %slice.16 = f32[4,6,192]{2,1,0:T(8,128)S(1)} slice(f32[4,80,256]{2,1,0:T(8,128)} %get-tuple-element.16), slice={[0:4], [40:46], [0:192]} | slice | bytes 36864 | tf_op jit(solution)/shard_map/slice | solution.py:480
  70.5 0.6 copy.22
  71.1 1.5 %slice.18 = f32[4,16,192]{2,1,0:T(8,128)} slice(f32[4,80,256]{2,1,0:T(8,128)} %get-tuple-element.16), slice={[0:4], [56:72], [0:192]} | slice | bytes 98304 | tf_op jit(solution)/shard_map/slice | solution.py:482
  72.6 0.9 %slice_bitcast_fusion = f32[4,192,38]{1,2,0:T(8,128)S(1)} fusion(f32[4,80,256]{2,1,0:T(8,128)} %get-tuple-element.16), kind=kLoop, calls=%fused_computation | loop fusion | bytes 233472 | tf_op jit(solution)/shard_map/transpose | solution.py:479
  73.5 0.0 copy-start
  73.5 0.7 copy.21
  74.3 0.2 copy-done
  74.4 0.6 copy.28
Async XLA Ops:
  73.5 0.9 %copy-start = (bf16[192,256]{1,0:T(8,128)(2,1)S(1)}, bf16[192,256]{1,0:T(8,128)(2,1)}, u32[]{:S(2)}) copy-start(bf16[192,256]{1,0:T(8,128)(2,1)} %get-tuple-element.15) | copy-start | bytes 294916
